TPU v7x, 512 devices: a whole 4x4x16 slice. The times are simulated.
512 devices in a mesh: rep: 32 (over z_lo, y, core), fsdp: 16 (over z_hi, x).
Axes of the slice: x: 4, y: 4, z: 16 (z_hi: 4, z_lo: 4; z = z_hi * 4 + z_lo), core: 2. Of those that a mesh axis runs over, the one named last changes fastest.
Arguments:
- inputs: bfloat16 [2, 65536, 4096], P(None, ('rep', 'fsdp')), may hold values from -3000 to 3000
- cotangent: bfloat16 [2, 65536, 512], P(None, ('rep', 'fsdp')), may hold values from -6 to 6
- weight: float32 [32, 4096, 512], P('rep', 'fsdp'), may hold values from -6 to 6
- norm_gain: float32 [32, 4096], P('rep', 'fsdp'), may hold values from 0.5 to 1.5
- adam_first: bfloat16 [32, 4096, 512], P('rep', 'fsdp'), may hold values from -0.00059890747 to 0.00059890747
- adam_second: bfloat16 [32, 4096, 512], P('rep', 'fsdp'), may hold values from 9.95351e-09 to 9.9651515e-08
- gain_first: float32 [32, 4096], P('rep', 'fsdp'), may hold values from -0.006 to 0.006
- gain_second: float32 [32, 4096], P('rep', 'fsdp'), may hold values from 1e-05 to 0.0001
- anchor_weight: float32 [4096, 512], P('fsdp'), may hold values from -6 to 6
- anchor_gain: float32 [4096], P('fsdp'), may hold values from 0.5 to 1.5
- outer_weight: float32 [4096, 512], P('fsdp'), may hold values from -3 to 3
- outer_gain: float32 [4096], P('fsdp'), may hold values from -0.3 to 0.3
Outputs:
- merged_weight: float32 [32, 4096, 512], P('rep', 'fsdp')
- merged_gain: float32 [32, 4096], P('rep', 'fsdp')
All inputs are finite; a program needn't handle non-finite values.
Results may differ from a plain program's by a relative error of at most 0.007.
Values may be sent and summed in bfloat16 or wider, within the bound.
A program may use at most 64 MiB of HBM per device.

v0:
```python
import jax
import jax.numpy as jnp
from jax import lax
from jax.sharding import PartitionSpec as P

INNER = 2


BETA_ONE = 0.9
BETA_TWO = 0.999
EPS_ADAM = 1e-08
RATE = 0.3
DECAY = 0.1
EPS_NORM = 1e-05
OUTER_RATE = 0.7
MOMENTUM = 0.9
MIXING = 0.5


def inverse_rms(values):
    widened = values.astype(jnp.float32)
    return lax.rsqrt(jnp.mean(widened * widened, axis=-1) + EPS_NORM)


def adam_update(current, gradient, moment_one, moment_two, decay_rate):
    moment_one = BETA_ONE * moment_one + (1.0 - BETA_ONE) * gradient
    moment_two = BETA_TWO * moment_two + (1.0 - BETA_TWO) * gradient * gradient
    current = current - RATE * (
        moment_one / (jnp.sqrt(moment_two) + EPS_ADAM) + decay_rate * current
    )
    return (current, moment_one, moment_two)


def outer_step(anchor, momentum, mean_delta):
    velocity = MOMENTUM * momentum + mean_delta
    return anchor - OUTER_RATE * (mean_delta + MOMENTUM * velocity)


def on_device(
    inputs,
    cotangent,
    weight,
    norm_gain,
    adam_first,
    adam_second,
    gain_first,
    gain_second,
    anchor_weight,
    anchor_gain,
    outer_weight,
    outer_gain,
):
    replicas = lax.axis_size("rep")
    current = weight[0]
    gain_now = norm_gain[0]
    delta_weight = anchor_weight - current
    delta_gain = anchor_gain - gain_now
    sum_weight, sum_gain = lax.psum((delta_weight, delta_gain), "rep")
    new_weight = outer_step(anchor_weight, outer_weight, sum_weight / replicas)
    new_gain = outer_step(anchor_gain, outer_gain, sum_gain / replicas)
    scale_rows = inverse_rms(inputs)
    columns = lax.all_to_all(inputs, "fsdp", split_axis=2, concat_axis=1, tiled=True)
    cotangents, scales_all = (
        lax.all_gather(cotangent, "fsdp", axis=1, tiled=True),
        lax.all_gather(scale_rows.astype(jnp.bfloat16), "fsdp", axis=1, tiled=True).astype(
            scale_rows.dtype
        ),
    )
    moment_one = adam_first[0].astype(jnp.float32)
    moment_two = adam_second[0].astype(jnp.float32)
    gain_one = gain_first[0]
    gain_two = gain_second[0]
    for inner_step in range(INNER):
        normed = columns[inner_step].astype(jnp.float32) * scales_all[inner_step][:, None]
        hidden = (normed * gain_now[None, :]).astype(jnp.bfloat16)
        grad_weight = lax.dot_general(
            hidden,
            cotangents[inner_step],
            (((0,), (0,)), ((), ())),
            preferred_element_type=jnp.float32,
        )
        weight_low = current.astype(jnp.bfloat16)
        local_grads = cotangent[inner_step]
        back_local = lax.dot_general(
            local_grads,
            lax.all_gather(weight_low, "fsdp", axis=0, tiled=True),
            (((1,), (1,)), ((), ())),
            preferred_element_type=jnp.float32,
        )
        normed_local = inputs[inner_step].astype(jnp.float32) * scale_rows[inner_step][:, None]
        partial_value = jnp.sum(normed_local * back_local, axis=0)
        grad_gain = lax.psum_scatter(partial_value, "fsdp", scatter_dimension=0, tiled=True)
        squares = lax.psum(
            jnp.sum(grad_weight * grad_weight) + jnp.sum(grad_gain * grad_gain), "fsdp"
        )
        factor = jnp.minimum(1.0, 1.0 / (jnp.sqrt(squares) + 1e-06))
        current, moment_one, moment_two = adam_update(
            current, factor * grad_weight, moment_one, moment_two, DECAY
        )
        gain_now, gain_one, gain_two = adam_update(
            gain_now, factor * grad_gain, gain_one, gain_two, 0.0
        )
    merged_weight = MIXING * current + (1.0 - MIXING) * new_weight
    merged_gain = MIXING * gain_now + (1.0 - MIXING) * new_gain
    return (merged_weight[None], merged_gain[None])


def solution(mesh):
    return jax.shard_map(
        on_device,
        mesh=mesh,
        in_specs=(
            P(None, ("rep", "fsdp"), None),
            P(None, ("rep", "fsdp"), None),
            P("rep", "fsdp", None),
            P("rep", "fsdp"),
            P("rep", "fsdp", None),
            P("rep", "fsdp", None),
            P("rep", "fsdp"),
            P("rep", "fsdp"),
            P("fsdp", None),
            P("fsdp"),
            P("fsdp", None),
            P("fsdp"),
        ),
        out_specs=(P("rep", "fsdp", None), P("rep", "fsdp")),
        check_vma=False,
    )
```

profile of v0, /device:TPU:1, one launch (start us, length us, event | category | flops | bytes accessed | tf_op | source)
XLA Modules:
  0.0 852.1 jit_solution(2452745179682893405)
XLA Ops:
  7.2 1.8 bitcast_convert_fusion
  9.0 6.2 copy.19
  15.2 18.4 %all-to-all-start = ((bf16[2,128,4096]{1,0,2:T(2,128)(2,1)}), bf16[2,128,4096]{1,0,2:T(2,128)(2,1)}, u32[]{:S(2)}, u32[]{:S(2)}) async-start(bf16[2,128,4096]{1,0,2:T(2,128)(2,1)} %copy.19), calls=%async_computation | async-start | bytes 4194304 | tf_op jit(solution)/shard_map/all_to_all | solution.py:62
  33.7 0.7 all-gather.4.cloned.1.call-update
  34.4 1.3 dynamic-slice
  36.3 0.5 multiply_reduce_fusion
  36.8 142.2 %all_gather.12 = bf16[2,2048]{1,0:T(2,128)(2,1)S(1)} all-gather(bf16[2,128]{1,0:T(2,128)(2,1)S(1)} %get-tuple-element.10), channel_id=1, replica_groups=mesh['rep'=32,'fsdp'=16] {'fsdp'}, dimensions={1}, use_global_device_ids=true | all-gather | bytes 8704 | tf_op jit(solution)/shard_map/all_gather | solution.py:65
  179.1 1.9 copy.20
  181.0 1.4 copy-done.1
  182.3 0.4 multiply_convert_fusion.1
  182.7 1.3 copy.21
  184.0 52.2 %all-gather.6.cloned.1.call-done = bf16[4096,512]{1,0:T(8,128)(2,1)} async-done(((bf16[256,512]{1,0:T(8,128)(2,1)}), bf16[4096,512]{1,0:T(8,128)(2,1)}) %all-gather.6.cloned.1.call-update) | async-done | bytes 4194320 | tf_op jit(solution)/shard_map/all_gather | solution.py:86
  236.3 3.7 fusion.3
  239.9 91.8 %all-reduce = f32[4096]{0:T(1024)S(1)} all-reduce(f32[4096]{0:T(1024)S(1)} %fusion.3), channel_id=2, replica_groups=mesh['rep'=32,'fsdp'=16] {'fsdp'}, use_global_device_ids=true, to_apply=%region_3.0.clone | all-reduce | flops 4096 | bytes 32768
  331.8 0.7 multiply_reduce_fusion.4
  332.5 34.5 %all-gather.4.cloned.1.call-done = bf16[2,2048,512]{2,1,0:T(8,128)(2,1)} async-done(((bf16[2,128,512]{2,1,0:T(8,128)(2,1)}), bf16[2,2048,512]{2,1,0:T(8,128)(2,1)}) %all-gather.4.cloned.1.call-update) | async-done | bytes 4194320 | tf_op jit(solution)/shard_map/all_gather | solution.py:64
  366.9 4.1 multiply_reduce_fusion.2
  372.4 48.1 %psum.28 = f32[]{:T(128)} all-reduce(f32[]{:T(128)S(6)} %add.100), channel_id=1, replica_groups=mesh['rep'=32,'fsdp'=16] {'fsdp'}, use_global_device_ids=true, to_apply=%region_5.0 | all-reduce | flops 1 | bytes 8 | tf_op jit(solution)/shard_map/psum | solution.py:93
  421.3 2.4 fusion.26
  423.8 0.1 fusion.28
  423.9 2.6 multiply_convert_fusion
  426.5 2.3 copy.22
  428.9 4.1 multiply_reduce_fusion.1
  432.9 124.1 %all-gather.8.cloned.1.call-done = bf16[4096,512]{1,0:T(8,128)(2,1)} async-done(((bf16[256,512]{1,0:T(8,128)(2,1)}), bf16[4096,512]{1,0:T(8,128)(2,1)}) %all-gather.8.cloned.1.call-update) | async-done | bytes 4194320 | tf_op jit(solution)/shard_map/all_gather | solution.py:86
  557.0 3.7 fusion.4
  560.7 82.3 %all-reduce.1 = f32[4096]{0:T(1024)S(1)} all-reduce(f32[4096]{0:T(1024)S(1)} %fusion.4), channel_id=3, replica_groups=mesh['rep'=32,'fsdp'=16] {'fsdp'}, use_global_device_ids=true, to_apply=%region_8.0.clone | all-reduce | flops 4096 | bytes 32768
  643.0 0.7 multiply_reduce_fusion.3
  645.1 81.3 %psum.31 = f32[256]{0:T(256)S(1)} all-reduce(f32[256]{0:T(256)S(1)} %get-tuple-element.6), channel_id=1, replica_groups=mesh['rep'=32,'fsdp'=16] {'rep'}, use_global_device_ids=true, to_apply=%region_12.0 | all-reduce | flops 256 | bytes 2048 | tf_op jit(solution)/shard_map/psum | solution.py:58
  726.4 39.8 %psum.29 = f32[]{:T(128)} all-reduce(f32[]{:T(128)S(6)} %add.110), channel_id=1, replica_groups=mesh['rep'=32,'fsdp'=16] {'fsdp'}, use_global_device_ids=true, to_apply=%region_10.0 | all-reduce | flops 1 | bytes 8 | tf_op jit(solution)/shard_map/psum | solution.py:93
  766.9 0.7 add_multiply_fusion
  767.6 74.7 %all-reduce.4.cloned.1.call-done = f32[256,512]{1,0:T(8,128)} async-done(((f32[256,512]{1,0:T(8,128)}), f32[256,512]{1,0:T(8,128)}) %all-reduce.4.cloned.1.call-update) | async-done | bytes 524304 | tf_op jit(solution)/shard_map/psum | solution.py:58
  842.2 3.3 multiply_bitcast_fusion
  (34 shorter events, 0.3 us)
Async XLA Ops:
  7.2 229.1 %all-gather.6.cloned.1.call-start = ((), (), s32[]{:S(2)}) async-start(), calls=%async_computation.2 | async-start | bytes 4456448 | tf_op jit(solution)/shard_map/all_gather | solution.py:86
  15.2 21.1 %copy-start = (bf16[2,128,4096]{2,1,0:T(8,128)(2,1)S(1)}, bf16[2,128,4096]{2,1,0:T(8,128)(2,1)}, u32[]{:S(2)}) copy-start(bf16[2,128,4096]{2,1,0:T(8,128)(2,1)} %param.12) | copy-start | bytes 6291460
  15.2 163.9 %all-to-all-start = ((bf16[2,128,4096]{1,0,2:T(2,128)(2,1)}), bf16[2,128,4096]{1,0,2:T(2,128)(2,1)}, u32[]{:S(2)}, u32[]{:S(2)}) async-start(bf16[2,128,4096]{1,0,2:T(2,128)(2,1)} %copy.19), calls=%async_computation | async-start | bytes 4194304 | tf_op jit(solution)/shard_map/all_to_all | solution.py:62
  33.6 333.3 %all-gather.4.cloned.1.call-start = ((), (), s32[]{:S(2)}) async-start(), calls=%async_computation.1 | async-start | bytes 4456448 | tf_op jit(solution)/shard_map/all_gather | solution.py:64
  34.4 522.6 %all-gather.8.cloned.1.call-start = ((), (), s32[]{:S(2)}) async-start(), calls=%async_computation.3 | async-start | bytes 4456448 | tf_op jit(solution)/shard_map/all_gather | solution.py:86
  179.1 3.3 copy-start.6
  180.9 1.4 copy-start.1
  182.3 53.9 %copy-start.5 = (bf16[2,128,512]{2,1,0:T(8,128)(2,1)S(1)}, bf16[2,128,512]{2,1,0:T(8,128)(2,1)}, u32[]{:S(2)}) copy-start(bf16[2,128,512]{2,1,0:T(8,128)(2,1)} %param.13) | copy-start | bytes 786436
  366.9 54.3 %copy-start.2 = (f32[1,256,512]{2,1,0:T(8,128)S(1)}, f32[1,256,512]{2,1,0:T(8,128)}, u32[]{:S(2)}) copy-start(f32[1,256,512]{2,1,0:T(8,128)} %param.14) | copy-start | bytes 1572868
  366.9 54.3 %copy-start.3 = (f32[256,512]{1,0:T(8,128)S(1)}, f32[256,512]{1,0:T(8,128)}, u32[]{:S(2)}) copy-start(f32[256,512]{1,0:T(8,128)} %param.20) | copy-start | bytes 1572868
  366.9 54.4 %copy-start.4 = (bf16[1,256,512]{2,1,0:T(8,128)(2,1)S(1)}, bf16[1,256,512]{2,1,0:T(8,128)(2,1)}, u32[]{:S(2)}) copy-start(bf16[1,256,512]{2,1,0:T(8,128)(2,1)} %param.17) | copy-start | bytes 786436
  371.1 52.7 %copy-start.8 = (f32[1,256]{1,0:T(1,128)S(1)}, f32[1,256]{1,0:T(1,128)}, u32[]{:S(2)}) copy-start(f32[1,256]{1,0:T(1,128)} %param.18) | copy-start | bytes 3076
  371.1 52.7 %copy-start.9 = (f32[1,256]{1,0:T(1,128)S(1)}, f32[1,256]{1,0:T(1,128)}, u32[]{:S(2)}) copy-start(f32[1,256]{1,0:T(1,128)} %param.19) | copy-start | bytes 3076
  371.1 52.7 %copy-start.7 = (f32[256]{0:T(256)S(1)}, f32[256]{0:T(256)}, u32[]{:S(2)}) copy-start(f32[256]{0:T(256)} %param.21) | copy-start | bytes 3076
  423.7 418.5 %all-reduce.4.cloned.1.call-start = ((), (), s32[]{:S(2)}) async-start(), calls=%async_computation.4 | async-start | bytes 1048576 | tf_op jit(solution)/shard_map/psum | solution.py:58
  557.0 209.9 %copy-start.10 = (f32[256]{0:T(256)S(1)}, f32[256]{0:T(256)}, u32[]{:S(2)}) copy-start(f32[256]{0:T(256)} %param.23) | copy-start | bytes 3076
Sparse Core Ops, SparseCore 0:
  11.6 224.6 all-gather.5
  239.3 127.6 all-gather.3
  423.8 133.1 all-gather.7
  559.8 282.4 all-reduce.3
where the time goes:
time: 853 us; the launch traced here: 852 us
  blocking collectives  486 us (57%)
  waiting for transfers between devices  286 us (34%)
  between operations  18.7 us (2%)
  starting transfers between devices  18.5 us (2%)
  matrix products  15.6 us (2%)
  local copies, waits for them, and re-layouts  14.4 us (2%)
  other arithmetic  13.1 us (2%)
    all_gather x2, waiting for transfers between devices, on_device(): lax.all_gather(weight_low, 'fsdp', axis=0, tiled=True)  176 us
    unnamed x2, blocking collectives  174 us
    all_gather x1, blocking collectives, on_device(): lax.all_gather(scale_rows.astype(jnp.bfloat16), 'fsdp', axis=1, tiled=True)  142 us
    psum x2, blocking collectives, on_device(): lax.psum(jnp.sum(grad_weight * grad_weight) + jnp.sum(grad_gain * grad_ga...  87.9 us
    psum x1, blocking collectives, on_device(): sum_weight, sum_gain = lax.psum((delta_weight, delta_gain), 'rep')  81.3 us
    psum x1, waiting for transfers between devices, on_device(): sum_weight, sum_gain = lax.psum((delta_weight, delta_gain), 'rep')  74.7 us
    all_gather x1, waiting for transfers between devices, on_device(): lax.all_gather(cotangent, 'fsdp', axis=1, tiled=True)  34.5 us
    all_to_all x1, starting transfers between devices, on_device(): lax.all_to_all(inputs, 'fsdp', split_axis=2, concat_axis=1, tiled=True)  18.4 us
  transfers between devices with their start and end apart: 5, of which 4 were waited for; matrix products, arithmetic and copies ran while one was open for 4% of the time, Pallas kernels for 0%

commit v1 on v0

v1 whole, which is shorter than its diff:
```python
import jax
import jax.numpy as jnp
from jax import lax
from jax.experimental import pallas as pl
from jax.experimental.pallas import tpu as pltpu
from jax.sharding import PartitionSpec as P

BETA_ONE = 0.9
BETA_TWO = 0.999
EPS_ADAM = 1e-08
RATE = 0.3
DECAY = 0.1
EPS_NORM = 1e-05
OUTER_RATE = 0.7
MOMENTUM = 0.9
MIXING = 0.5

INNER = 2
NX = 4
NZ = 4
NF = NX * NZ
TOK = 128
ROWS = 256
HALF = ROWS // 2
D = ROWS * NF
KW = 512
ORDER = (2, 1, 3, 0)

MESH = pl.DeviceIdType.MESH


def flip(value, bits):
    if bits == 0:
        return value
    if bits == 1:
        return value + 1 - 2 * (value % 2)
    if bits == 2:
        return (value + 2) % 4
    return 3 - value


def adam_update(current, gradient, moment_one, moment_two, decay_rate):
    moment_one = BETA_ONE * moment_one + (1.0 - BETA_ONE) * gradient
    moment_two = BETA_TWO * moment_two + (1.0 - BETA_TWO) * gradient * gradient
    current = current - RATE * (
        moment_one / (jnp.sqrt(moment_two) + EPS_ADAM) + decay_rate * current
    )
    return (current, moment_one, moment_two)


def outer_step(anchor, momentum, mean_delta):
    velocity = MOMENTUM * momentum + mean_delta
    return anchor - OUTER_RATE * (mean_delta + MOMENTUM * velocity)


def kernel(
    inputs,
    cotangent,
    weight,
    adam_first,
    adam_second,
    gains,
    out_weight,
    out_gain,
    xin,
    cin,
    win,
    m_one,
    m_two,
    columns,
    scaled,
    grads,
    keep,
    z_out,
    z_in,
    norms,
    local_sem,
    x_send,
    x_recv,
    c_send,
    c_recv,
    z_send,
    z_recv,
    q_send,
    q_recv,
):
    me = lax.axis_index("fsdp")
    my_z = me // NX
    my_x = me % NX

    def at(z, x):
        return {"fsdp": z * NX + x}

    loads = []
    for place, (source, target) in enumerate(
        (
            (inputs.at[0], xin.at[0]),
            (cotangent, cin),
            (inputs.at[1], xin.at[1]),
            (weight, win),
            (adam_first, m_one),
            (adam_second, m_two),
        )
    ):
        copy = pltpu.make_async_copy(source, target, local_sem.at[place])
        copy.start()
        loads.append(copy)

    def column(j, i):
        owner = flip(my_z, j) * NX + flip(my_x, i)
        return pl.ds(pl.multiple_of(owner * ROWS, ROWS), ROWS)

    own_copies = {}
    place = len(loads)
    for s in range(INNER):
        for j in ORDER:
            copy = pltpu.make_async_copy(
                inputs.at[s, :, column(j, 0)],
                columns.at[s, j, pl.ds(0, TOK)],
                local_sem.at[place],
            )
            copy.start()
            own_copies[s, j] = copy
            place += 1

    barrier = pltpu.get_barrier_semaphore()
    for k in range(1, NF):
        pl.semaphore_signal(
            barrier, inc=1, device_id={"fsdp": (me + k) % NF}, device_id_type=MESH
        )
    pl.semaphore_wait(barrier, NF - 1)

    sends = []

    def send(source, target, send_sem, recv_sem, device):
        copy = pltpu.make_async_remote_copy(
            src_ref=source,
            dst_ref=target,
            send_sem=send_sem,
            recv_sem=recv_sem,
            device_id=device,
            device_id_type=MESH,
        )
        copy.start()
        sends.append(copy)
        return copy

    x_copies = {}
    c_copies = {}
    z_copies = {}
    q_copies = {}

    def send_columns(s, j):
        x_copies[s, j] = [
            send(
                inputs.at[s, :, column(j, i)],
                columns.at[s, j, pl.ds(i * TOK, TOK)],
                x_send.at[s, j, i - 1],
                x_recv.at[s, j, i - 1],
                at(my_z, flip(my_x, i)),
            )
            for i in (1, 3, 2)
        ]

    def send_scaled(s):
        values = xin[s].astype(jnp.float32)
        mean = jnp.mean(values * values, axis=-1, keepdims=True)
        scale = lax.rsqrt(mean + EPS_NORM)
        scaled[s, pl.ds(0, TOK), :] = (cin[s].astype(jnp.float32) * scale).astype(
            jnp.bfloat16
        )
        c_copies[s] = [
            send(
                scaled.at[s, pl.ds(0, TOK)],
                scaled.at[s, pl.ds(i * TOK, TOK)],
                c_send.at[s, i - 1],
                c_recv.at[s, i - 1],
                at(my_z, flip(my_x, i)),
            )
            for i in (1, 3, 2)
        ]

    def send_rows(s, slot, j):
        z_copies[s, slot] = send(
            z_out.at[s, slot],
            z_in.at[s, slot],
            z_send.at[s, slot],
            z_recv.at[s, slot],
            at(flip(my_z, j), my_x),
        )

    chunks = [(s, j) for s in range(INNER) for j in ORDER]
    send_columns(*chunks[0])
    loads[0].wait()
    loads[1].wait()
    send_scaled(0)
    send_columns(*chunks[1])
    loads[2].wait()

    low = pl.ds(0, HALF)
    high = pl.ds(HALF, HALF)

    def product(number):
        s, j = chunks[number]
        own_copies[s, j].wait()
        for copy in x_copies[s, j]:
            copy.wait_recv()
        if j == ORDER[0]:
            for copy in c_copies[s]:
                copy.wait_recv()
        if number + 2 < len(chunks):
            send_columns(*chunks[number + 2])
            if number == 1:
                send_scaled(1)
        block = lax.dot_general(
            columns[s, j],
            scaled[s],
            (((0,), (0,)), ((), ())),
            preferred_element_type=jnp.float32,
        )
        if j == 2:
            z_out[s, 0] = block[:HALF].astype(jnp.bfloat16)
            send_rows(s, 0, 1)
            z_out[s, 1] = block[HALF:].astype(jnp.bfloat16)
            send_rows(s, 1, 3)
        elif j == 1:
            z_out[s, 2] = block[:HALF].astype(jnp.bfloat16)
            send_rows(s, 2, 1)
            keep[s, 1] = block[HALF:]
        elif j == 3:
            z_out[s, 3] = block[HALF:].astype(jnp.bfloat16)
            send_rows(s, 3, 3)
            keep[s, 0] = block[:HALF]
        else:
            grads[s] = block

    def forward(s):
        z_copies[s, 0].wait_recv()
        z_out[s, 4] = (keep[s, 0] + z_in[s, 0].astype(jnp.float32)).astype(jnp.bfloat16)
        send_rows(s, 4, 3)
        z_copies[s, 1].wait_recv()
        z_out[s, 5] = (keep[s, 1] + z_in[s, 1].astype(jnp.float32)).astype(jnp.bfloat16)
        send_rows(s, 5, 1)

    def reduce_rows(s):
        for slot in (2, 3, 4, 5):
            z_copies[s, slot].wait_recv()
        grads[s, low] = grads[s, low] + (
            z_in[s, 2].astype(jnp.float32) + z_in[s, 4].astype(jnp.float32)
        )
        grads[s, high] = grads[s, high] + (
            z_in[s, 3].astype(jnp.float32) + z_in[s, 5].astype(jnp.float32)
        )

    def update(s, current, gain, moments, gain_moments):
        product_sum = grads[s]
        low_weight = current.astype(jnp.bfloat16).astype(jnp.float32)
        grad_gain = jnp.sum(product_sum * low_weight, axis=1, keepdims=True)
        grad_weight = product_sum * gain
        squares = grad_weight * grad_weight
        folded = squares[:, 0:128] + squares[:, 128:256] + squares[:, 256:384] + squares[:, 384:512]
        lane = lax.broadcasted_iota(jnp.int32, (ROWS, 128), 1)
        folded = folded + jnp.where(lane == 0, grad_gain * grad_gain, 0.0)
        norms[s, 0] = jnp.sum(folded.reshape(ROWS // 8, 8, 128), axis=0)
        q_copies[s] = [
            send(
                norms.at[s, 0],
                norms.at[s, k],
                q_send.at[s, k - 1],
                q_recv.at[s, k - 1],
                {"fsdp": (me + k) % NF},
            )
            for k in range(1, NF)
        ]
        for copy in q_copies[s]:
            copy.wait_recv()
        total = jnp.sum(jnp.sum(norms[s], axis=0), keepdims=True)
        factor = jnp.minimum(1.0, 1.0 / (jnp.sqrt(total) + 1e-06))
        current, one, two = adam_update(
            current, factor * grad_weight, moments[0], moments[1], DECAY
        )
        gain, gain_one, gain_two = adam_update(
            gain, factor * grad_gain, gain_moments[0], gain_moments[1], 0.0
        )
        return current, gain, (one, two), (gain_one, gain_two)

    for number in range(len(ORDER)):
        product(number)
    forward(0)
    for number in range(len(ORDER), 2 * len(ORDER)):
        product(number)
    for copy in loads[3:]:
        copy.wait()
    turned = jnp.transpose(gains[...])
    reduce_rows(0)
    current, gain, moments, gain_moments = update(
        0,
        win[...],
        turned[:, 0:1],
        (m_one[...].astype(jnp.float32), m_two[...].astype(jnp.float32)),
        (turned[:, 1:2], turned[:, 2:3]),
    )
    forward(1)
    reduce_rows(1)
    current, gain, _, _ = update(1, current, gain, moments, gain_moments)
    out_weight[...] = current
    out_gain[...] = jnp.transpose(jnp.broadcast_to(gain, (ROWS, 8)))
    for copy in sends:
        copy.wait_send()


def window(inputs, cotangent, weight, adam_first, adam_second, gains):
    anywhere = pl.BlockSpec(memory_space=pl.ANY)
    vmem = pl.BlockSpec(memory_space=pltpu.VMEM)
    dma = pltpu.SemaphoreType.DMA
    f32, bf16 = jnp.float32, jnp.bfloat16
    return pl.pallas_call(
        kernel,
        out_shape=(
            jax.ShapeDtypeStruct((ROWS, KW), f32),
            jax.ShapeDtypeStruct((8, ROWS), f32),
        ),
        in_specs=[anywhere] * 5 + [vmem],
        out_specs=(vmem, vmem),
        scratch_shapes=[
            pltpu.VMEM((INNER, TOK, D), bf16),
            pltpu.VMEM((INNER, TOK, KW), bf16),
            pltpu.VMEM((ROWS, KW), f32),
            pltpu.VMEM((ROWS, KW), bf16),
            pltpu.VMEM((ROWS, KW), bf16),
            pltpu.VMEM((INNER, NZ, NX * TOK, ROWS), bf16),
            pltpu.VMEM((INNER, NX * TOK, KW), bf16),
            pltpu.VMEM((INNER, ROWS, KW), f32),
            pltpu.VMEM((INNER, 2, HALF, KW), f32),
            pltpu.VMEM((INNER, 6, HALF, KW), bf16),
            pltpu.VMEM((INNER, 6, HALF, KW), bf16),
            pltpu.VMEM((INNER, NF, 8, 128), f32),
            dma((6 + INNER * NZ,)),
            dma((INNER, NZ, NX - 1)),
            dma((INNER, NZ, NX - 1)),
            dma((INNER, NX - 1)),
            dma((INNER, NX - 1)),
            dma((INNER, 6)),
            dma((INNER, 6)),
            dma((INNER, NF - 1)),
            dma((INNER, NF - 1)),
        ],
        compiler_params=pltpu.CompilerParams(
            collective_id=0, has_side_effects=True, vmem_limit_bytes=40 * 1024 * 1024
        ),
        cost_estimate=pl.CostEstimate(
            flops=4 * INNER * NX * TOK * NZ * ROWS * KW,
            bytes_accessed=8 * 1024 * 1024,
            transcendentals=0,
        ),
        name="inner_window",
    )(inputs, cotangent, weight, adam_first, adam_second, gains)


def on_device(
    inputs,
    cotangent,
    weight,
    norm_gain,
    adam_first,
    adam_second,
    gain_first,
    gain_second,
    anchor_weight,
    anchor_gain,
    outer_weight,
    outer_gain,
):
    replicas = lax.axis_size("rep")
    sum_weight, sum_gain = lax.psum(
        (anchor_weight - weight[0], anchor_gain - norm_gain[0]), "rep"
    )
    gains = jnp.concatenate(
        (norm_gain, gain_first, gain_second, jnp.zeros((5, ROWS), jnp.float32)), axis=0
    )
    current, gain_now = window(
        inputs, cotangent, weight[0], adam_first[0], adam_second[0], gains
    )
    new_weight = outer_step(anchor_weight, outer_weight, sum_weight / replicas)
    new_gain = outer_step(anchor_gain, outer_gain, sum_gain / replicas)
    merged_weight = MIXING * current + (1.0 - MIXING) * new_weight
    merged_gain = MIXING * gain_now[0] + (1.0 - MIXING) * new_gain
    return (merged_weight[None], merged_gain[None])


def solution(mesh):
    return jax.shard_map(
        on_device,
        mesh=mesh,
        in_specs=(
            P(None, ("rep", "fsdp"), None),
            P(None, ("rep", "fsdp"), None),
            P("rep", "fsdp", None),
            P("rep", "fsdp"),
            P("rep", "fsdp", None),
            P("rep", "fsdp", None),
            P("rep", "fsdp"),
            P("rep", "fsdp"),
            P("fsdp", None),
            P("fsdp"),
            P("fsdp", None),
            P("fsdp"),
        ),
        out_specs=(P("rep", "fsdp", None), P("rep", "fsdp")),
        check_vma=False,
    )
```

time: 853 us -> 336 us (0.39)
  blocking collectives: 486 us -> 71.8 us
  waiting for transfers between devices: 286 us -> 130 us
  Pallas kernels: 0 us -> 113 us
  starting transfers between devices: 18.5 us -> 0.04 us
  matrix products: 15.6 us -> 0 us
  local copies, waits for them, and re-layouts: 14.4 us -> 1.71 us
    all_gather x3 -> x0, waiting for transfers between devices: 211 us -> none  [the longest x2 176 us: on_device(): lax.all_gather(weight_low, 'fsdp', axis=0, tiled=True)]
    unnamed x2 -> x0, blocking collectives: 174 us -> none
    all_gather x1 -> x0, blocking collectives: 142 us -> none  [on_device(): lax.all_gather(scale_rows.astype(jnp.bfloat16), 'fsdp', axis=1, tiled=True)]
    pallas_call x0 -> x1, Pallas kernels: none -> 113 us  [window(): pl.pallas_call(kernel, out_shape=(jax.ShapeDtypeStruct((ROWS, KW), f32),...]
    psum x3 -> x1, blocking collectives: 169 us -> 71.8 us  [on_device(): lax.psum((anchor_weight - weight[0], anchor_gain - norm_gain[0]), 'rep')]
    psum x1, waiting for transfers between devices: 74.7 us -> 130 us  [on_device(): lax.psum((anchor_weight - weight[0], anchor_gain - norm_gain[0]), 'rep')]
    all_to_all x1 -> x0, starting transfers between devices: 18.4 us -> none  [on_device(): lax.all_to_all(inputs, 'fsdp', split_axis=2, concat_axis=1, tiled=True)]
    dot_general x4 -> x0, matrix products: 15.6 us -> none  [the longest x2 8.2 us: on_device(): lax.dot_general(hidden, cotangents[inner_step], (((0,), (0,)), ((), ())),...]
  transfers between devices with their start and end apart: 5 -> 1, of which waited for: 4 -> 1; matrix products, arithmetic and copies ran while one was open for 4% -> 0% of each run, Pallas kernels for 0% -> 34%
where the time goes in v1:
time: 336 us; the launch traced here: 335 us
  waiting for transfers between devices  130 us (39%)
  Pallas kernels  113 us (34%)
  blocking collectives  71.8 us (21%)
  between operations  14.1 us (4%)
  other arithmetic  4.9 us (1%)
    psum x1, waiting for transfers between devices, on_device(): lax.psum((anchor_weight - weight[0], anchor_gain - norm_gain[0]), 'rep')  130 us
    pallas_call x1, Pallas kernels, window(): pl.pallas_call(kernel, out_shape=(jax.ShapeDtypeStruct((ROWS, KW), f32),...  113 us
    psum x1, blocking collectives, on_device(): lax.psum((anchor_weight - weight[0], anchor_gain - norm_gain[0]), 'rep')  71.8 us
  transfers between devices with their start and end apart: 1, of which 1 were waited for; matrix products, arithmetic and copies ran while one was open for 0% of the time, Pallas kernels for 34%

profile of v1, /device:TPU:1, one launch (start us, length us, event | category | flops | bytes accessed | tf_op | source)
XLA Modules:
  0.0 335.4 jit_solution(8953133025414987826)
XLA Ops:
  7.2 0.0 copy-start
  7.2 0.0 copy-start.7
  7.2 0.0 copy-start.10
  7.2 0.0 copy-start.9
  7.2 0.0 copy-start.3
  7.2 0.0 copy-start.4
  7.2 0.0 copy-start.2
  7.2 0.0 all-reduce.2.cloned.1.call-start
  7.3 2.2 bitcast_subtract_fusion
  9.5 0.0 all-reduce.2.cloned.1.call-update
  9.5 0.1 pad.3.clone
  9.6 0.0 copy-done.7
  9.6 0.0 copy-done.10
  9.6 0.0 copy-done.9
  9.6 0.1 maximum_maximum_fusion.gains
  9.6 0.0 copy-done
  9.7 0.0 copy-done.3
  9.7 0.0 copy-done.4
  9.7 0.0 copy-done.2
  9.7 0.0 copy-start.1
  9.7 1.6 copy-done.1
  11.3 0.0 copy-start.8
  11.3 0.0 copy-start.11
  11.3 112.8 %inner_window.1 = (f32[256,512]{1,0:T(8,128)S(1)}, f32[8,256]{1,0:T(8,128)S(1)}) custom-call(bf16[2,128,4096]{2,1,0:T(8,128)(2,1)S(1)} %copy-done.1, bf16[2,128,512]{2,1,0:T(8,128)(2,1)S(1)} %copy-done.2, f32[256,512]{1,0:T(8,128)S(1)} %bitcast.9, bf16[256,512]{1,0:T(8,128)(2,1)S(1)} %bitcast.10, bf16[256,512]{1,0:T(8,128)(2,1)S(1)} %bitcast.11, ...), custom_call_target="tpu_custom_call" | custom-call | flops 2147483648 | bytes 8388608 | tf_op jit(solution)/shard_map/inner_window/pallas_call | solution.py:317
  124.1 0.0 copy-done.8
  124.2 71.8 %psum.15 = f32[256]{0:T(256)S(1)} all-reduce(f32[256]{0:T(256)S(1)} %sub.14), channel_id=1, replica_groups=mesh['rep'=32,'fsdp'=16] {'rep'}, use_global_device_ids=true, to_apply=%region_1.0 | all-reduce | flops 256 | bytes 2048 | tf_op jit(solution)/shard_map/psum | solution.py:375
  195.9 0.0 copy-done.11
  195.9 0.6 add_multiply_fusion
  196.5 130.0 %all-reduce.2.cloned.1.call-done = f32[256,512]{1,0:T(8,128)} async-done(((f32[256,512]{1,0:T(8,128)}), f32[256,512]{1,0:T(8,128)}) %all-reduce.2.cloned.1.call-update) | async-done | bytes 524304 | tf_op jit(solution)/shard_map/psum | solution.py:375
  326.5 0.0 copy-done.5
  326.5 0.0 copy-done.6
  326.5 2.1 multiply_bitcast_fusion
  (5 shorter events, 0.0 us)
Async XLA Ops:
  7.2 2.5 copy-start
  7.2 2.4 copy-start.7
  7.2 2.4 copy-start.10
  7.2 2.4 copy-start.9
  7.2 2.4 copy-start.3
  7.2 2.4 copy-start.4
  7.2 2.4 copy-start.2
  7.2 319.3 %all-reduce.2.cloned.1.call-start = ((), (), s32[]{:S(2)}) async-start(), calls=%async_computation | async-start | bytes 1048576 | tf_op jit(solution)/shard_map/psum | solution.py:375
  9.7 1.6 copy-start.1
  11.3 112.9 %copy-start.8 = (f32[256]{0:T(256)S(1)}, f32[256]{0:T(256)}, u32[]{:S(2)}) copy-start(f32[256]{0:T(256)} %param.21) | copy-start | bytes 3076
  11.3 184.7 %copy-start.11 = (f32[256]{0:T(256)S(1)}, f32[256]{0:T(256)}, u32[]{:S(2)}) copy-start(f32[256]{0:T(256)} %param.23) | copy-start | bytes 3076
  11.3 315.2 %copy-start.5 = (f32[256,512]{1,0:T(8,128)S(1)}, f32[256,512]{1,0:T(8,128)}, u32[]{:S(2)}) copy-start(f32[256,512]{1,0:T(8,128)} %param.20) | copy-start | bytes 1572868
  11.3 315.2 %copy-start.6 = (f32[256,512]{1,0:T(8,128)S(1)}, f32[256,512]{1,0:T(8,128)}, u32[]{:S(2)}) copy-start(f32[256,512]{1,0:T(8,128)} %param.22) | copy-start | bytes 1572868
Sparse Core Ops, SparseCore 0:
  11.5 314.9 all-reduce.1

commit v2 on v1

--- a/solution.py
+++ b/solution.py
@@ -24,6 +24,10 @@
 HALF = ROWS // 2
 D = ROWS * NF
 KW = 512
+NP = 8
+NL = 4
+PART = ROWS // NP
+SUB = PART // NL
 ORDER = (2, 1, 3, 0)
 
 MESH = pl.DeviceIdType.MESH
@@ -59,6 +63,8 @@
     weight,
     adam_first,
     adam_second,
+    anchor_weight,
+    outer_weight,
     gains,
     out_weight,
     out_gain,
@@ -74,6 +80,14 @@
     z_out,
     z_in,
     norms,
+    parts,
+    part_sum,
+    subs,
+    merged,
+    anchor_rows,
+    outer_rows,
+    gain_parts,
+    gain_subs,
     local_sem,
     x_send,
     x_recv,
@@ -83,13 +97,32 @@
     z_recv,
     q_send,
     q_recv,
+    p_send,
+    p_recv,
+    l_send,
+    l_recv,
 ):
+    replicas = NP * NL
+    rep = lax.axis_index("rep")
+    my_part = rep % NP
+    my_plane = rep // NP
     me = lax.axis_index("fsdp")
     my_z = me // NX
     my_x = me % NX
 
     def at(z, x):
         return {"fsdp": z * NX + x}
+
+    def in_plane(k):
+        return {"rep": my_plane * NP + (my_part + k) % NP}
+
+    def over_planes(k):
+        return {"rep": (my_plane + k) % NL * NP + my_part}
+
+    def part_of(part):
+        return pl.ds(pl.multiple_of(part * PART, PART), PART)
+
+    sub_rows = pl.ds(pl.multiple_of(my_part * PART + my_plane * SUB, SUB), SUB)
 
     loads = []
     for place, (source, target) in enumerate(
@@ -100,6 +133,8 @@
             (weight, win),
             (adam_first, m_one),
             (adam_second, m_two),
+            (anchor_weight.at[sub_rows], anchor_rows),
+            (outer_weight.at[sub_rows], outer_rows),
         )
     ):
         copy = pltpu.make_async_copy(source, target, local_sem.at[place])
@@ -128,7 +163,11 @@
         pl.semaphore_signal(
             barrier, inc=1, device_id={"fsdp": (me + k) % NF}, device_id_type=MESH
         )
-    pl.semaphore_wait(barrier, NF - 1)
+    for k in range(1, NP):
+        pl.semaphore_signal(barrier, inc=1, device_id=in_plane(k), device_id_type=MESH)
+    for k in range(1, NL):
+        pl.semaphore_signal(barrier, inc=1, device_id=over_planes(k), device_id_type=MESH)
+    pl.semaphore_wait(barrier, NF + NP + NL - 3)
 
     sends = []
 
@@ -189,8 +228,89 @@
             at(flip(my_z, j), my_x),
         )
 
+
+    def exchange(stage, sems, count, source, target, device):
+        return [
+            send(
+                source(k),
+                target(k),
+                sems[0].at[stage, k - 1],
+                sems[1].at[stage, k - 1],
+                device(k),
+            )
+            for k in range(1, count)
+        ]
+
+    planes = (p_send, p_recv), NP
+    levels = (l_send, l_recv), NL
+
+    def rep_start():
+        return exchange(
+            0,
+            *planes,
+            lambda k: weight.at[part_of((my_part + k) % NP)],
+            lambda k: parts.at[k],
+            in_plane,
+        ) + exchange(1, *planes, lambda k: gains, lambda k: gain_parts.at[k], in_plane)
+
+    def rep_second(copies):
+        for copy in copies:
+            copy.wait_recv()
+        loads[3].wait()
+        total = win[part_of(my_part), :]
+        for k in range(1, NP):
+            total = total + parts[k]
+        part_sum[...] = total
+        gain_total = gains[...]
+        for k in range(1, NP):
+            gain_total = gain_total + gain_parts[k]
+        gain_subs[0] = gain_total
+        return exchange(
+            0,
+            *levels,
+            lambda k: part_sum.at[
+                pl.ds(pl.multiple_of((my_plane + k) % NL * SUB, SUB), SUB)
+            ],
+            lambda k: subs.at[k],
+            over_planes,
+        ) + exchange(
+            1, *levels, lambda k: gain_subs.at[0], lambda k: gain_subs.at[k], over_planes
+        )
+
+    def rep_third(copies):
+        for copy in copies:
+            copy.wait_recv()
+        total = part_sum[pl.ds(pl.multiple_of(my_plane * SUB, SUB), SUB), :]
+        for k in range(1, NL):
+            total = total + subs[k]
+        loads[6].wait()
+        loads[7].wait()
+        anchor = anchor_rows[...]
+        merged[sub_rows, :] = outer_step(
+            anchor, outer_rows[...], anchor - total / replicas
+        )
+        return exchange(
+            2,
+            *levels,
+            lambda k: merged.at[sub_rows],
+            lambda k: merged.at[sub_rows],
+            over_planes,
+        )
+
+    def rep_fourth(copies):
+        for copy in copies:
+            copy.wait_recv()
+        return exchange(
+            2,
+            *planes,
+            lambda k: merged.at[part_of(my_part)],
+            lambda k: merged.at[part_of(my_part)],
+            in_plane,
+        )
+
     chunks = [(s, j) for s in range(INNER) for j in ORDER]
     send_columns(*chunks[0])
+    rep_copies = rep_start()
     loads[0].wait()
     loads[1].wait()
     send_scaled(0)
@@ -284,12 +404,19 @@
         )
         return current, gain, (one, two), (gain_one, gain_two)
 
-    for number in range(len(ORDER)):
-        product(number)
+    product(0)
+    product(1)
+    rep_copies = rep_second(rep_copies)
+    product(2)
+    product(3)
     forward(0)
-    for number in range(len(ORDER), 2 * len(ORDER)):
-        product(number)
-    for copy in loads[3:]:
+    rep_copies = rep_third(rep_copies)
+    product(4)
+    product(5)
+    rep_copies = rep_fourth(rep_copies)
+    product(6)
+    product(7)
+    for copy in loads[4:6]:
         copy.wait()
     turned = jnp.transpose(gains[...])
     reduce_rows(0)
@@ -303,13 +430,23 @@
     forward(1)
     reduce_rows(1)
     current, gain, _, _ = update(1, current, gain, moments, gain_moments)
-    out_weight[...] = current
-    out_gain[...] = jnp.transpose(jnp.broadcast_to(gain, (ROWS, 8)))
+    for copy in rep_copies:
+        copy.wait_recv()
+    out_weight[...] = MIXING * current + (1.0 - MIXING) * merged[...]
+    gain_total = gain_subs[0] + gain_subs[1] + gain_subs[2] + gain_subs[3]
+    anchor_gain = gains[3:4, :]
+    new_gain = outer_step(
+        anchor_gain, gains[4:5, :], anchor_gain - gain_total[0:1, :] / replicas
+    )
+    gain_row = jnp.transpose(jnp.broadcast_to(gain, (ROWS, 8)))
+    out_gain[...] = MIXING * gain_row[0:1, :] + (1.0 - MIXING) * new_gain
     for copy in sends:
         copy.wait_send()
 
 
-def window(inputs, cotangent, weight, adam_first, adam_second, gains):
+def window(
+    inputs, cotangent, weight, adam_first, adam_second, anchor_weight, outer_weight, gains
+):
     anywhere = pl.BlockSpec(memory_space=pl.ANY)
     vmem = pl.BlockSpec(memory_space=pltpu.VMEM)
     dma = pltpu.SemaphoreType.DMA
@@ -318,9 +455,9 @@
         kernel,
         out_shape=(
             jax.ShapeDtypeStruct((ROWS, KW), f32),
-            jax.ShapeDtypeStruct((8, ROWS), f32),
+            jax.ShapeDtypeStruct((1, ROWS), f32),
         ),
-        in_specs=[anywhere] * 5 + [vmem],
+        in_specs=[anywhere] * 7 + [vmem],
         out_specs=(vmem, vmem),
         scratch_shapes=[
             pltpu.VMEM((INNER, TOK, D), bf16),
@@ -335,7 +472,15 @@
             pltpu.VMEM((INNER, 6, HALF, KW), bf16),
             pltpu.VMEM((INNER, 6, HALF, KW), bf16),
             pltpu.VMEM((INNER, NF, 8, 128), f32),
-            dma((6 + INNER * NZ,)),
+            pltpu.VMEM((NP, PART, KW), f32),
+            pltpu.VMEM((PART, KW), f32),
+            pltpu.VMEM((NL, SUB, KW), f32),
+            pltpu.VMEM((ROWS, KW), f32),
+            pltpu.VMEM((SUB, KW), f32),
+            pltpu.VMEM((SUB, KW), f32),
+            pltpu.VMEM((NP, 8, ROWS), f32),
+            pltpu.VMEM((NL, 8, ROWS), f32),
+            dma((8 + INNER * NZ,)),
             dma((INNER, NZ, NX - 1)),
             dma((INNER, NZ, NX - 1)),
             dma((INNER, NX - 1)),
@@ -344,6 +489,10 @@
             dma((INNER, 6)),
             dma((INNER, NF - 1)),
             dma((INNER, NF - 1)),
+            dma((3, NP - 1)),
+            dma((3, NP - 1)),
+            dma((3, NL - 1)),
+            dma((3, NL - 1)),
         ],
         compiler_params=pltpu.CompilerParams(
             collective_id=0, has_side_effects=True, vmem_limit_bytes=40 * 1024 * 1024
@@ -354,7 +503,9 @@
             transcendentals=0,
         ),
         name="inner_window",
-    )(inputs, cotangent, weight, adam_first, adam_second, gains)
+    )(
+        inputs, cotangent, weight, adam_first, adam_second, anchor_weight, outer_weight, gains
+    )
 
 
 def on_device(
@@ -371,21 +522,28 @@
     outer_weight,
     outer_gain,
 ):
-    replicas = lax.axis_size("rep")
-    sum_weight, sum_gain = lax.psum(
-        (anchor_weight - weight[0], anchor_gain - norm_gain[0]), "rep"
-    )
     gains = jnp.concatenate(
-        (norm_gain, gain_first, gain_second, jnp.zeros((5, ROWS), jnp.float32)), axis=0
-    )
-    current, gain_now = window(
-        inputs, cotangent, weight[0], adam_first[0], adam_second[0], gains
-    )
-    new_weight = outer_step(anchor_weight, outer_weight, sum_weight / replicas)
-    new_gain = outer_step(anchor_gain, outer_gain, sum_gain / replicas)
-    merged_weight = MIXING * current + (1.0 - MIXING) * new_weight
-    merged_gain = MIXING * gain_now[0] + (1.0 - MIXING) * new_gain
-    return (merged_weight[None], merged_gain[None])
+        (
+            norm_gain,
+            gain_first,
+            gain_second,
+            anchor_gain[None],
+            outer_gain[None],
+            jnp.zeros((3, ROWS), jnp.float32),
+        ),
+        axis=0,
+    )
+    merged_weight, merged_gain = window(
+        inputs,
+        cotangent,
+        weight[0],
+        adam_first[0],
+        adam_second[0],
+        anchor_weight,
+        outer_weight,
+        gains,
+    )
+    return (merged_weight[None], merged_gain)
 
 
 def solution(mesh):

time: 336 us -> 134 us (0.40)
  the two profiles are of different devices: /device:TPU:1 before, /device:TPU:96 now
where the time goes in v2:
time: 134 us; the launch traced here: 133 us
  Pallas kernels  123 us (92%)
  local copies, waits for them, and re-layouts  9.68 us (7%)
    pallas_call x1, Pallas kernels, window(): pl.pallas_call(kernel, out_shape=(jax.ShapeDtypeStruct((ROWS, KW), f32),...  123 us
    unnamed x16, local copies, waits for them, and re-layouts  8.91 us

profile of v2, /device:TPU:96, one launch (start us, length us, event | category | flops | bytes accessed | tf_op | source)
XLA Modules:
  0.0 133.2 jit_solution(10990684166662699167)
XLA Ops:
  0.6 0.8 concatenate.3.gains
  1.4 0.0 copy-start
  1.4 1.6 %copy-done = bf16[2,128,4096]{2,1,0:T(8,128)(2,1)S(1)} copy-done((bf16[2,128,4096]{2,1,0:T(8,128)(2,1)S(1)}, bf16[2,128,4096]{2,1,0:T(8,128)(2,1)}, u32[]{:S(2)}) %copy-start) | copy-done | bytes 2097176
  3.0 0.0 copy-start.1
  3.0 1.0 copy-done.1
  4.0 0.0 copy-start.2
  4.0 1.0 copy-done.2
  5.1 0.0 copy-start.3
  5.1 1.0 copy-done.3
  6.1 0.0 copy-start.4
  6.1 0.9 copy-done.4
  7.1 0.0 copy-start.5
  7.1 0.9 copy-done.5
  8.0 0.0 copy-start.6
  8.0 0.9 copy-done.6
  9.0 122.9 %inner_window.1 = (f32[256,512]{1,0:T(8,128)S(1)}, f32[1,256]{1,0:T(1,128)S(1)}) custom-call(bf16[2,128,4096]{2,1,0:T(8,128)(2,1)S(1)} %copy-done, bf16[2,128,512]{2,1,0:T(8,128)(2,1)S(1)} %copy-done.4, f32[256,512]{1,0:T(8,128)S(1)} %bitcast.7, bf16[256,512]{1,0:T(8,128)(2,1)S(1)} %bitcast.8, bf16[256,512]{1,0:T(8,128)(2,1)S(1)} %bitcast.9, ...), custom_call_target="tpu_custom_call" | custom-call | flops 2147483648 | bytes 8388608 | tf_op jit(solution)/shard_map/inner_window/pallas_call | solution.py:454
  131.9 0.8 copy.16
  132.7 0.6 copy.17
  (1 shorter events, 0.0 us)
Async XLA Ops:
  1.4 1.6 %copy-start = (bf16[2,128,4096]{2,1,0:T(8,128)(2,1)S(1)}, bf16[2,128,4096]{2,1,0:T(8,128)(2,1)}, u32[]{:S(2)}) copy-start(bf16[2,128,4096]{2,1,0:T(8,128)(2,1)} %inputs.1) | copy-start | bytes 6291460
  3.0 1.0 copy-start.1
  4.0 1.0 copy-start.2
  5.1 1.0 copy-start.3
  6.1 0.9 copy-start.4
  7.1 0.9 copy-start.5
  8.0 0.9 copy-start.6

commit v3 on v2

--- a/solution.py
+++ b/solution.py
@@ -65,7 +65,11 @@
     adam_second,
     anchor_weight,
     outer_weight,
-    gains,
+    norm_gain,
+    gain_first,
+    gain_second,
+    anchor_gain,
+    outer_gain,
     out_weight,
     out_gain,
     xin,
@@ -86,6 +90,8 @@
     merged,
     anchor_rows,
     outer_rows,
+    gain_in,
+    gains,
     gain_parts,
     gain_subs,
     local_sem,
@@ -135,6 +141,11 @@
             (adam_second, m_two),
             (anchor_weight.at[sub_rows], anchor_rows),
             (outer_weight.at[sub_rows], outer_rows),
+            (norm_gain, gain_in.at[0]),
+            (gain_first, gain_in.at[1]),
+            (gain_second, gain_in.at[2]),
+            (anchor_gain, gain_in.at[3]),
+            (outer_gain, gain_in.at[4]),
         )
     ):
         copy = pltpu.make_async_copy(source, target, local_sem.at[place])
@@ -310,6 +321,11 @@
 
     chunks = [(s, j) for s in range(INNER) for j in ORDER]
     send_columns(*chunks[0])
+    for copy in loads[8:]:
+        copy.wait()
+    gains[...] = jnp.concatenate(
+        [gain_in[k] for k in range(5)] + [jnp.zeros((3, ROWS), jnp.float32)], axis=0
+    )
     rep_copies = rep_start()
     loads[0].wait()
     loads[1].wait()
@@ -433,10 +449,12 @@
     for copy in rep_copies:
         copy.wait_recv()
     out_weight[...] = MIXING * current + (1.0 - MIXING) * merged[...]
-    gain_total = gain_subs[0] + gain_subs[1] + gain_subs[2] + gain_subs[3]
-    anchor_gain = gains[3:4, :]
+    gain_total = gain_subs[0]
+    for k in range(1, NL):
+        gain_total = gain_total + gain_subs[k]
+    anchor_row = gains[3:4, :]
     new_gain = outer_step(
-        anchor_gain, gains[4:5, :], anchor_gain - gain_total[0:1, :] / replicas
+        anchor_row, gains[4:5, :], anchor_row - gain_total[0:1, :] / replicas
     )
     gain_row = jnp.transpose(jnp.broadcast_to(gain, (ROWS, 8)))
     out_gain[...] = MIXING * gain_row[0:1, :] + (1.0 - MIXING) * new_gain
@@ -444,9 +462,7 @@
         copy.wait_send()
 
 
-def window(
-    inputs, cotangent, weight, adam_first, adam_second, anchor_weight, outer_weight, gains
-):
+def window(*operands):
     anywhere = pl.BlockSpec(memory_space=pl.ANY)
     vmem = pl.BlockSpec(memory_space=pltpu.VMEM)
     dma = pltpu.SemaphoreType.DMA
@@ -457,7 +473,7 @@
             jax.ShapeDtypeStruct((ROWS, KW), f32),
             jax.ShapeDtypeStruct((1, ROWS), f32),
         ),
-        in_specs=[anywhere] * 7 + [vmem],
+        in_specs=[anywhere] * len(operands),
         out_specs=(vmem, vmem),
         scratch_shapes=[
             pltpu.VMEM((INNER, TOK, D), bf16),
@@ -478,9 +494,11 @@
             pltpu.VMEM((ROWS, KW), f32),
             pltpu.VMEM((SUB, KW), f32),
             pltpu.VMEM((SUB, KW), f32),
+            pltpu.VMEM((5, 1, ROWS), f32),
+            pltpu.VMEM((8, ROWS), f32),
             pltpu.VMEM((NP, 8, ROWS), f32),
             pltpu.VMEM((NL, 8, ROWS), f32),
-            dma((8 + INNER * NZ,)),
+            dma((13 + INNER * NZ,)),
             dma((INNER, NZ, NX - 1)),
             dma((INNER, NZ, NX - 1)),
             dma((INNER, NX - 1)),
@@ -495,7 +513,7 @@
             dma((3, NL - 1)),
         ],
         compiler_params=pltpu.CompilerParams(
-            collective_id=0, has_side_effects=True, vmem_limit_bytes=40 * 1024 * 1024
+            collective_id=0, has_side_effects=True, vmem_limit_bytes=60 * 1024 * 1024
         ),
         cost_estimate=pl.CostEstimate(
             flops=4 * INNER * NX * TOK * NZ * ROWS * KW,
@@ -503,9 +521,7 @@
             transcendentals=0,
         ),
         name="inner_window",
-    )(
-        inputs, cotangent, weight, adam_first, adam_second, anchor_weight, outer_weight, gains
-    )
+    )(*operands)
 
 
 def on_device(
@@ -522,17 +538,6 @@
     outer_weight,
     outer_gain,
 ):
-    gains = jnp.concatenate(
-        (
-            norm_gain,
-            gain_first,
-            gain_second,
-            anchor_gain[None],
-            outer_gain[None],
-            jnp.zeros((3, ROWS), jnp.float32),
-        ),
-        axis=0,
-    )
     merged_weight, merged_gain = window(
         inputs,
         cotangent,
@@ -541,7 +546,11 @@
         adam_second[0],
         anchor_weight,
         outer_weight,
-        gains,
+        norm_gain,
+        gain_first,
+        gain_second,
+        anchor_gain[None],
+        outer_gain[None],
     )
     return (merged_weight[None], merged_gain)
 

time: 134 us -> 127 us (0.948)
  local copies, waits for them, and re-layouts: 9.68 us -> 3.07 us
    unnamed x16 -> x2, local copies, waits for them, and re-layouts: 8.91 us -> 3.07 us
where the time goes in v3:
time: 127 us
  Pallas kernels  124 us (98%)
  local copies, waits for them, and re-layouts  3.07 us (2%)
    pallas_call x1, Pallas kernels, window(): pl.pallas_call(kernel, out_shape=(jax.ShapeDtypeStruct((ROWS, KW), f32),...  124 us
    unnamed x2, local copies, waits for them, and re-layouts  3.07 us

profile of v3, /device:TPU:96, one launch (start us, length us, event | category | flops | bytes accessed | tf_op | source)
XLA Modules:
  0.0 127.3 jit_solution(15203422415347301200)
XLA Ops:
  0.6 123.6 %inner_window.1 = (f32[256,512]{1,0:T(8,128)}, f32[1,256]{1,0:T(1,128)}) custom-call(bf16[2,128,4096]{2,1,0:T(8,128)(2,1)} %inputs.1, bf16[2,128,512]{2,1,0:T(8,128)(2,1)} %cotangent.1, f32[256,512]{1,0:T(8,128)} %bitcast.7, bf16[256,512]{1,0:T(8,128)(2,1)} %bitcast.8, bf16[256,512]{1,0:T(8,128)(2,1)} %bitcast.9, f32[256,512]{1,0:T(8,128)} %anchor_weight.1, ...), custom_call_target="tpu_custom_call" | custom-call | flops 2147483648 | bytes 8388608 | tf_op jit(solution)/shard_map/inner_window/pallas_call | solution.py:470
  124.2 1.9 %copy.16 = f32[1,256,512]{2,1,0:T(8,128)} copy(f32[1,256,512]{2,1,0:T(8,128)} %bitcast.6) | data formatting | bytes 1048576
  126.1 1.2 copy.17

commit v4 on v3

--- a/solution.py
+++ b/solution.py
@@ -125,6 +125,16 @@
     def over_planes(k):
         return {"rep": (my_plane + k) % NL * NP + my_part}
 
+    barrier = pltpu.get_barrier_semaphore()
+    for k in range(1, NF):
+        pl.semaphore_signal(
+            barrier, inc=1, device_id={"fsdp": (me + k) % NF}, device_id_type=MESH
+        )
+    for k in range(1, NP):
+        pl.semaphore_signal(barrier, inc=1, device_id=in_plane(k), device_id_type=MESH)
+    for k in range(1, NL):
+        pl.semaphore_signal(barrier, inc=1, device_id=over_planes(k), device_id_type=MESH)
+
     def part_of(part):
         return pl.ds(pl.multiple_of(part * PART, PART), PART)
 
@@ -169,17 +179,6 @@
             own_copies[s, j] = copy
             place += 1
 
-    barrier = pltpu.get_barrier_semaphore()
-    for k in range(1, NF):
-        pl.semaphore_signal(
-            barrier, inc=1, device_id={"fsdp": (me + k) % NF}, device_id_type=MESH
-        )
-    for k in range(1, NP):
-        pl.semaphore_signal(barrier, inc=1, device_id=in_plane(k), device_id_type=MESH)
-    for k in range(1, NL):
-        pl.semaphore_signal(barrier, inc=1, device_id=over_planes(k), device_id_type=MESH)
-    pl.semaphore_wait(barrier, NF + NP + NL - 3)
-
     sends = []
 
     def send(source, target, send_sem, recv_sem, device):
@@ -212,32 +211,43 @@
             for i in (1, 3, 2)
         ]
 
-    def send_scaled(s):
+    def scale(s):
         values = xin[s].astype(jnp.float32)
         mean = jnp.mean(values * values, axis=-1, keepdims=True)
         scale = lax.rsqrt(mean + EPS_NORM)
         scaled[s, pl.ds(0, TOK), :] = (cin[s].astype(jnp.float32) * scale).astype(
             jnp.bfloat16
         )
-        c_copies[s] = [
+
+    def send_scaled(s, part, width):
+        columns_of = pl.ds(part * width, width)
+        c_copies[s, part] = [
             send(
-                scaled.at[s, pl.ds(0, TOK)],
-                scaled.at[s, pl.ds(i * TOK, TOK)],
-                c_send.at[s, i - 1],
-                c_recv.at[s, i - 1],
+                scaled.at[s, pl.ds(0, TOK), columns_of],
+                scaled.at[s, pl.ds(i * TOK, TOK), columns_of],
+                c_send.at[s, part, i - 1],
+                c_recv.at[s, part, i - 1],
                 at(my_z, flip(my_x, i)),
             )
             for i in (1, 3, 2)
         ]
 
-    def send_rows(s, slot, j):
-        z_copies[s, slot] = send(
-            z_out.at[s, slot],
-            z_in.at[s, slot],
-            z_send.at[s, slot],
-            z_recv.at[s, slot],
+    def send_rows(s, slot, j, part=0, width=KW):
+        columns_of = pl.ds(part * width, width)
+        sem = slot + 6 * part
+        z_copies[s, sem] = send(
+            z_out.at[s, slot, :, columns_of],
+            z_in.at[s, slot, :, columns_of],
+            z_send.at[s, sem],
+            z_recv.at[s, sem],
             at(flip(my_z, j), my_x),
         )
+
+    def sent(s, *slots):
+        for slot in slots:
+            copy = z_copies[s, slot]
+            copy.wait_send()
+            sends[:] = [other for other in sends if other is not copy]
 
 
     def exchange(stage, sems, count, source, target, device):
@@ -262,7 +272,9 @@
             lambda k: weight.at[part_of((my_part + k) % NP)],
             lambda k: parts.at[k],
             in_plane,
-        ) + exchange(1, *planes, lambda k: gains, lambda k: gain_parts.at[k], in_plane)
+        ) + exchange(
+            1, *planes, lambda k: gain_in.at[0], lambda k: gain_parts.at[k], in_plane
+        )
 
     def rep_second(copies):
         for copy in copies:
@@ -272,7 +284,7 @@
         for k in range(1, NP):
             total = total + parts[k]
         part_sum[...] = total
-        gain_total = gains[...]
+        gain_total = gain_in[0]
         for k in range(1, NP):
             gain_total = gain_total + gain_parts[k]
         gain_subs[0] = gain_total
@@ -319,64 +331,57 @@
             in_plane,
         )
 
-    chunks = [(s, j) for s in range(INNER) for j in ORDER]
-    send_columns(*chunks[0])
-    for copy in loads[8:]:
-        copy.wait()
-    gains[...] = jnp.concatenate(
-        [gain_in[k] for k in range(5)] + [jnp.zeros((3, ROWS), jnp.float32)], axis=0
-    )
-    rep_copies = rep_start()
-    loads[0].wait()
-    loads[1].wait()
-    send_scaled(0)
-    send_columns(*chunks[1])
-    loads[2].wait()
-
     low = pl.ds(0, HALF)
     high = pl.ds(HALF, HALF)
 
-    def product(number):
-        s, j = chunks[number]
-        own_copies[s, j].wait()
-        for copy in x_copies[s, j]:
-            copy.wait_recv()
-        if j == ORDER[0]:
-            for copy in c_copies[s]:
-                copy.wait_recv()
-        if number + 2 < len(chunks):
-            send_columns(*chunks[number + 2])
-            if number == 1:
-                send_scaled(1)
-        block = lax.dot_general(
+    def multiply(s, j, columns_of):
+        return lax.dot_general(
             columns[s, j],
-            scaled[s],
+            scaled[s, :, columns_of],
             (((0,), (0,)), ((), ())),
             preferred_element_type=jnp.float32,
         )
-        if j == 2:
-            z_out[s, 0] = block[:HALF].astype(jnp.bfloat16)
-            send_rows(s, 0, 1)
-            z_out[s, 1] = block[HALF:].astype(jnp.bfloat16)
-            send_rows(s, 1, 3)
-        elif j == 1:
+
+    def arrived(s, j, part=None):
+        if part in (None, 0):
+            own_copies[s, j].wait()
+            for copy in x_copies[s, j]:
+                copy.wait_recv()
+        if part is not None:
+            for copy in c_copies[s, part]:
+                copy.wait_recv()
+
+    def first_product(s, parts_of):
+        width = KW // parts_of
+        for part in range(parts_of):
+            arrived(s, 2, part)
+            columns_of = pl.ds(part * width, width)
+            block = multiply(s, 2, columns_of)
+            z_out[s, 0, :, columns_of] = block[:HALF].astype(jnp.bfloat16)
+            z_out[s, 1, :, columns_of] = block[HALF:].astype(jnp.bfloat16)
+            if s == 0:
+                send_rows(s, 0, 1, part, width)
+                send_rows(s, 1, 3, part, width)
+
+    def product(s, j):
+        arrived(s, j)
+        block = multiply(s, j, pl.ds(0, KW))
+        if j == 1:
             z_out[s, 2] = block[:HALF].astype(jnp.bfloat16)
-            send_rows(s, 2, 1)
             keep[s, 1] = block[HALF:]
         elif j == 3:
             z_out[s, 3] = block[HALF:].astype(jnp.bfloat16)
-            send_rows(s, 3, 3)
             keep[s, 0] = block[:HALF]
         else:
             grads[s] = block
 
     def forward(s):
-        z_copies[s, 0].wait_recv()
-        z_out[s, 4] = (keep[s, 0] + z_in[s, 0].astype(jnp.float32)).astype(jnp.bfloat16)
-        send_rows(s, 4, 3)
-        z_copies[s, 1].wait_recv()
-        z_out[s, 5] = (keep[s, 1] + z_in[s, 1].astype(jnp.float32)).astype(jnp.bfloat16)
-        send_rows(s, 5, 1)
+        for slot, target, j in ((0, 4, 3), (1, 5, 1)):
+            z_copies[s, slot].wait_recv()
+            z_copies[s, slot + 6].wait_recv()
+            total = keep[s, slot] + z_in[s, slot].astype(jnp.float32)
+            z_out[s, target] = total.astype(jnp.bfloat16)
+            send_rows(s, target, j)
 
     def reduce_rows(s):
         for slot in (2, 3, 4, 5):
@@ -388,7 +393,7 @@
             z_in[s, 3].astype(jnp.float32) + z_in[s, 5].astype(jnp.float32)
         )
 
-    def update(s, current, gain, moments, gain_moments):
+    def send_norm(s, current, gain):
         product_sum = grads[s]
         low_weight = current.astype(jnp.bfloat16).astype(jnp.float32)
         grad_gain = jnp.sum(product_sum * low_weight, axis=1, keepdims=True)
@@ -397,7 +402,7 @@
         folded = squares[:, 0:128] + squares[:, 128:256] + squares[:, 256:384] + squares[:, 384:512]
         lane = lax.broadcasted_iota(jnp.int32, (ROWS, 128), 1)
         folded = folded + jnp.where(lane == 0, grad_gain * grad_gain, 0.0)
-        norms[s, 0] = jnp.sum(folded.reshape(ROWS // 8, 8, 128), axis=0)
+        norms[s, 0] = jnp.sum(folded, axis=0, keepdims=True)
         q_copies[s] = [
             send(
                 norms.at[s, 0],
@@ -408,53 +413,97 @@
             )
             for k in range(1, NF)
         ]
+        return grad_gain
+
+    def update(s, current, gain, grad_gain, moments, gain_moments):
         for copy in q_copies[s]:
             copy.wait_recv()
         total = jnp.sum(jnp.sum(norms[s], axis=0), keepdims=True)
         factor = jnp.minimum(1.0, 1.0 / (jnp.sqrt(total) + 1e-06))
         current, one, two = adam_update(
-            current, factor * grad_weight, moments[0], moments[1], DECAY
+            current, factor * (grads[s] * gain), moments[0], moments[1], DECAY
         )
         gain, gain_one, gain_two = adam_update(
             gain, factor * grad_gain, gain_moments[0], gain_moments[1], 0.0
         )
         return current, gain, (one, two), (gain_one, gain_two)
 
-    product(0)
-    product(1)
+    pl.semaphore_wait(barrier, NF + NP + NL - 3)
+
+    send_columns(0, 2)
+    for copy in loads[:2]:
+        copy.wait()
+    scale(0)
+    send_scaled(0, 0, KW // 2)
+    send_scaled(0, 1, KW // 2)
+    for copy in loads[8:]:
+        copy.wait()
+    gains[...] = jnp.concatenate(
+        [gain_in[k] for k in range(5)] + [jnp.zeros((3, ROWS), jnp.float32)], axis=0
+    )
+    rep_copies = rep_start()
+    send_columns(0, 1)
+    first_product(0, 2)
+    send_columns(0, 3)
+    send_columns(0, 0)
+    product(0, 1)
+    send_rows(0, 2, 1)
+    loads[2].wait()
+    scale(1)
+    send_scaled(1, 0, KW)
+    send_columns(1, 2)
+    product(0, 3)
+    send_rows(0, 3, 3)
+    product(0, 0)
+    send_columns(1, 1)
+    send_columns(1, 3)
+    send_columns(1, 0)
     rep_copies = rep_second(rep_copies)
-    product(2)
-    product(3)
     forward(0)
+    first_product(1, 1)
     rep_copies = rep_third(rep_copies)
-    product(4)
-    product(5)
+    sent(0, 2, 3)
+    send_rows(1, 0, 1, 0, KW // 2)
+    send_rows(1, 1, 3, 0, KW // 2)
+    product(1, 1)
+    product(1, 3)
     rep_copies = rep_fourth(rep_copies)
-    product(6)
-    product(7)
+    product(1, 0)
     for copy in loads[4:6]:
         copy.wait()
     turned = jnp.transpose(gains[...])
+    current, gain = win[...], turned[:, 0:1]
+    sent(0, 4, 5)
     reduce_rows(0)
+    grad_gain = send_norm(0, current, gain)
+    send_rows(1, 0, 1, 1, KW // 2)
+    send_rows(1, 1, 3, 1, KW // 2)
+    send_rows(1, 2, 1)
+    send_rows(1, 3, 3)
+    forward(1)
     current, gain, moments, gain_moments = update(
         0,
-        win[...],
-        turned[:, 0:1],
+        current,
+        gain,
+        grad_gain,
         (m_one[...].astype(jnp.float32), m_two[...].astype(jnp.float32)),
         (turned[:, 1:2], turned[:, 2:3]),
     )
-    forward(1)
-    reduce_rows(1)
-    current, gain, _, _ = update(1, current, gain, moments, gain_moments)
     for copy in rep_copies:
         copy.wait_recv()
+    for copy in sends:
+        copy.wait_send()
+    sends.clear()
+    reduce_rows(1)
+    grad_gain = send_norm(1, current, gain)
+    current, gain, _, _ = update(1, current, gain, grad_gain, moments, gain_moments)
     out_weight[...] = MIXING * current + (1.0 - MIXING) * merged[...]
     gain_total = gain_subs[0]
     for k in range(1, NL):
         gain_total = gain_total + gain_subs[k]
     anchor_row = gains[3:4, :]
     new_gain = outer_step(
-        anchor_row, gains[4:5, :], anchor_row - gain_total[0:1, :] / replicas
+        anchor_row, gains[4:5, :], anchor_row - gain_total / replicas
     )
     gain_row = jnp.transpose(jnp.broadcast_to(gain, (ROWS, 8)))
     out_gain[...] = MIXING * gain_row[0:1, :] + (1.0 - MIXING) * new_gain
@@ -487,7 +536,7 @@
             pltpu.VMEM((INNER, 2, HALF, KW), f32),
             pltpu.VMEM((INNER, 6, HALF, KW), bf16),
             pltpu.VMEM((INNER, 6, HALF, KW), bf16),
-            pltpu.VMEM((INNER, NF, 8, 128), f32),
+            pltpu.VMEM((INNER, NF, 1, 128), f32),
             pltpu.VMEM((NP, PART, KW), f32),
             pltpu.VMEM((PART, KW), f32),
             pltpu.VMEM((NL, SUB, KW), f32),
@@ -496,15 +545,15 @@
             pltpu.VMEM((SUB, KW), f32),
             pltpu.VMEM((5, 1, ROWS), f32),
             pltpu.VMEM((8, ROWS), f32),
-            pltpu.VMEM((NP, 8, ROWS), f32),
-            pltpu.VMEM((NL, 8, ROWS), f32),
+            pltpu.VMEM((NP, 1, ROWS), f32),
+            pltpu.VMEM((NL, 1, ROWS), f32),
             dma((13 + INNER * NZ,)),
             dma((INNER, NZ, NX - 1)),
             dma((INNER, NZ, NX - 1)),
-            dma((INNER, NX - 1)),
-            dma((INNER, NX - 1)),
-            dma((INNER, 6)),
-            dma((INNER, 6)),
+            dma((INNER, 2, NX - 1)),
+            dma((INNER, 2, NX - 1)),
+            dma((INNER, 8)),
+            dma((INNER, 8)),
             dma((INNER, NF - 1)),
             dma((INNER, NF - 1)),
             dma((3, NP - 1)),

time: 127 us -> 116 us (0.913)
  the two profiles are of different devices: /device:TPU:96 before, /device:TPU:1 now
where the time goes in v4:
time: 116 us
  Pallas kernels  112 us (97%)
  local copies, waits for them, and re-layouts  3.07 us (3%)
    pallas_call x1, Pallas kernels, window(): pl.pallas_call(kernel, out_shape=(jax.ShapeDtypeStruct((ROWS, KW), f32),...  112 us
    unnamed x2, local copies, waits for them, and re-layouts  3.07 us

profile of v4, /device:TPU:1, one launch (start us, length us, event | category | flops | bytes accessed | tf_op | source)
XLA Modules:
  0.0 115.5 jit_solution(4799745039368342403)
XLA Ops:
  0.6 111.8 %inner_window.1 = (f32[256,512]{1,0:T(8,128)}, f32[1,256]{1,0:T(1,128)}) custom-call(bf16[2,128,4096]{2,1,0:T(8,128)(2,1)} %inputs.1, bf16[2,128,512]{2,1,0:T(8,128)(2,1)} %cotangent.1, f32[256,512]{1,0:T(8,128)} %bitcast.7, bf16[256,512]{1,0:T(8,128)(2,1)} %bitcast.8, bf16[256,512]{1,0:T(8,128)(2,1)} %bitcast.9, f32[256,512]{1,0:T(8,128)} %anchor_weight.1, ...), custom_call_target="tpu_custom_call" | custom-call | flops 2147483648 | bytes 8388608 | tf_op jit(solution)/shard_map/inner_window/pallas_call | solution.py:519
  112.5 1.9 %copy.16 = f32[1,256,512]{2,1,0:T(8,128)} copy(f32[1,256,512]{2,1,0:T(8,128)} %bitcast.6) | data formatting | bytes 1048576
  114.3 1.2 %copy.17 = f32[1,256]{1,0:T(1,128)} copy(f32[1,256]{1,0:T(1,128)} %get-tuple-element.9) | data formatting | bytes 2048

commit v5 on v4

--- a/solution.py
+++ b/solution.py
@@ -28,6 +28,7 @@
 NL = 4
 PART = ROWS // NP
 SUB = PART // NL
+PARTS = (4, 2)
 ORDER = (2, 1, 3, 0)
 
 MESH = pl.DeviceIdType.MESH
@@ -126,9 +127,9 @@
         return {"rep": (my_plane + k) % NL * NP + my_part}
 
     barrier = pltpu.get_barrier_semaphore()
-    for k in range(1, NF):
+    for j, i in ((0, 1), (0, 3), (0, 2), (1, 0), (3, 0)):
         pl.semaphore_signal(
-            barrier, inc=1, device_id={"fsdp": (me + k) % NF}, device_id_type=MESH
+            barrier, inc=1, device_id=at(flip(my_z, j), flip(my_x, i)), device_id_type=MESH
         )
     for k in range(1, NP):
         pl.semaphore_signal(barrier, inc=1, device_id=in_plane(k), device_id_type=MESH)
@@ -234,7 +235,7 @@
 
     def send_rows(s, slot, j, part=0, width=KW):
         columns_of = pl.ds(part * width, width)
-        sem = slot + 6 * part
+        sem = slot if part == 0 else 4 + 2 * part + slot
         z_copies[s, sem] = send(
             z_out.at[s, slot, :, columns_of],
             z_in.at[s, slot, :, columns_of],
@@ -378,7 +379,8 @@
     def forward(s):
         for slot, target, j in ((0, 4, 3), (1, 5, 1)):
             z_copies[s, slot].wait_recv()
-            z_copies[s, slot + 6].wait_recv()
+            for part in range(1, PARTS[s]):
+                z_copies[s, 4 + 2 * part + slot].wait_recv()
             total = keep[s, slot] + z_in[s, slot].astype(jnp.float32)
             z_out[s, target] = total.astype(jnp.bfloat16)
             send_rows(s, target, j)
@@ -428,14 +430,14 @@
         )
         return current, gain, (one, two), (gain_one, gain_two)
 
-    pl.semaphore_wait(barrier, NF + NP + NL - 3)
+    pl.semaphore_wait(barrier, 5 + NP + NL - 2)
 
     send_columns(0, 2)
     for copy in loads[:2]:
         copy.wait()
     scale(0)
-    send_scaled(0, 0, KW // 2)
-    send_scaled(0, 1, KW // 2)
+    for part in range(PARTS[0]):
+        send_scaled(0, part, KW // PARTS[0])
     for copy in loads[8:]:
         copy.wait()
     gains[...] = jnp.concatenate(
@@ -443,7 +445,7 @@
     )
     rep_copies = rep_start()
     send_columns(0, 1)
-    first_product(0, 2)
+    first_product(0, PARTS[0])
     send_columns(0, 3)
     send_columns(0, 0)
     product(0, 1)
@@ -550,10 +552,10 @@
             dma((13 + INNER * NZ,)),
             dma((INNER, NZ, NX - 1)),
             dma((INNER, NZ, NX - 1)),
-            dma((INNER, 2, NX - 1)),
-            dma((INNER, 2, NX - 1)),
-            dma((INNER, 8)),
-            dma((INNER, 8)),
+            dma((INNER, PARTS[0], NX - 1)),
+            dma((INNER, PARTS[0], NX - 1)),
+            dma((INNER, 4 + 2 * PARTS[0])),
+            dma((INNER, 4 + 2 * PARTS[0])),
             dma((INNER, NF - 1)),
             dma((INNER, NF - 1)),
             dma((3, NP - 1)),

time: 116 us -> 112 us (0.966)
  Pallas kernels: 112 us -> 107 us
    pallas_call x1, Pallas kernels: 112 us -> 107 us  [window(): pl.pallas_call(kernel, out_shape=(jax.ShapeDtypeStruct((ROWS, KW), f32),...]
where the time goes in v5:
time: 112 us; the launch traced here: 111 us
  Pallas kernels  107 us (96%)
  local copies, waits for them, and re-layouts  3.07 us (3%)
    pallas_call x1, Pallas kernels, window(): pl.pallas_call(kernel, out_shape=(jax.ShapeDtypeStruct((ROWS, KW), f32),...  107 us
    unnamed x2, local copies, waits for them, and re-layouts  3.07 us

profile of v5, /device:TPU:1, one launch (start us, length us, event | category | flops | bytes accessed | tf_op | source)
XLA Modules:
  0.0 110.9 jit_solution(16650027373410345592)
XLA Ops:
  0.6 107.1 %inner_window.1 = (f32[256,512]{1,0:T(8,128)}, f32[1,256]{1,0:T(1,128)}) custom-call(bf16[2,128,4096]{2,1,0:T(8,128)(2,1)} %inputs.1, bf16[2,128,512]{2,1,0:T(8,128)(2,1)} %cotangent.1, f32[256,512]{1,0:T(8,128)} %bitcast.7, bf16[256,512]{1,0:T(8,128)(2,1)} %bitcast.8, bf16[256,512]{1,0:T(8,128)(2,1)} %bitcast.9, f32[256,512]{1,0:T(8,128)} %anchor_weight.1, ...), custom_call_target="tpu_custom_call" | custom-call | flops 2147483648 | bytes 8388608 | tf_op jit(solution)/shard_map/inner_window/pallas_call | solution.py:521
  107.8 1.9 %copy.16 = f32[1,256,512]{2,1,0:T(8,128)} copy(f32[1,256,512]{2,1,0:T(8,128)} %bitcast.6) | data formatting | bytes 1048576
  109.7 1.2 %copy.17 = f32[1,256]{1,0:T(1,128)} copy(f32[1,256]{1,0:T(1,128)} %get-tuple-element.9) | data formatting | bytes 2048

commit v6 on v5

--- a/solution.py
+++ b/solution.py
@@ -30,6 +30,8 @@
 SUB = PART // NL
 PARTS = (4, 2)
 ORDER = (2, 1, 3, 0)
+
+FAR_FIRST = [(j, i) for j in (2, 1, 3, 0) for i in (2, 1, 3, 0) if i + j > 0]
 
 MESH = pl.DeviceIdType.MESH
 
@@ -411,9 +413,9 @@
                 norms.at[s, k],
                 q_send.at[s, k - 1],
                 q_recv.at[s, k - 1],
-                {"fsdp": (me + k) % NF},
+                at(flip(my_z, j), flip(my_x, i)),
             )
-            for k in range(1, NF)
+            for k, (j, i) in enumerate(FAR_FIRST, 1)
         ]
         return grad_gain
 
@@ -463,13 +465,12 @@
     rep_copies = rep_second(rep_copies)
     forward(0)
     first_product(1, 1)
-    rep_copies = rep_third(rep_copies)
     sent(0, 2, 3)
     send_rows(1, 0, 1, 0, KW // 2)
     send_rows(1, 1, 3, 0, KW // 2)
+    rep_copies = rep_third(rep_copies)
     product(1, 1)
     product(1, 3)
-    rep_copies = rep_fourth(rep_copies)
     product(1, 0)
     for copy in loads[4:6]:
         copy.wait()
@@ -483,6 +484,7 @@
     send_rows(1, 2, 1)
     send_rows(1, 3, 3)
     forward(1)
+    rep_copies = rep_fourth(rep_copies)
     current, gain, moments, gain_moments = update(
         0,
         current,

time: 112 us -> 111 us (level)
  the two profiles are of different devices: /device:TPU:1 before, /device:TPU:72 now
where the time goes in v6:
time: 111 us
  Pallas kernels  108 us (97%)
  local copies, waits for them, and re-layouts  3.07 us (3%)
    pallas_call x1, Pallas kernels, window(): pl.pallas_call(kernel, out_shape=(jax.ShapeDtypeStruct((ROWS, KW), f32),...  108 us
    unnamed x2, local copies, waits for them, and re-layouts  3.07 us

profile of v6, /device:TPU:72, one launch (start us, length us, event | category | flops | bytes accessed | tf_op | source)
XLA Modules:
  0.0 111.3 jit_solution(13602529184200052856)
XLA Ops:
  0.6 107.6 %inner_window.1 = (f32[256,512]{1,0:T(8,128)}, f32[1,256]{1,0:T(1,128)}) custom-call(bf16[2,128,4096]{2,1,0:T(8,128)(2,1)} %inputs.1, bf16[2,128,512]{2,1,0:T(8,128)(2,1)} %cotangent.1, f32[256,512]{1,0:T(8,128)} %bitcast.7, bf16[256,512]{1,0:T(8,128)(2,1)} %bitcast.8, bf16[256,512]{1,0:T(8,128)(2,1)} %bitcast.9, f32[256,512]{1,0:T(8,128)} %anchor_weight.1, ...), custom_call_target="tpu_custom_call" | custom-call | flops 2147483648 | bytes 8388608 | tf_op jit(solution)/shard_map/inner_window/pallas_call | solution.py:523
  108.2 1.9 %copy.16 = f32[1,256,512]{2,1,0:T(8,128)} copy(f32[1,256,512]{2,1,0:T(8,128)} %bitcast.6) | data formatting | bytes 1048576
  110.1 1.2 %copy.17 = f32[1,256]{1,0:T(1,128)} copy(f32[1,256]{1,0:T(1,128)} %get-tuple-element.9) | data formatting | bytes 2048

commit v7 on v6

--- a/solution.py
+++ b/solution.py
@@ -28,7 +28,7 @@
 NL = 4
 PART = ROWS // NP
 SUB = PART // NL
-PARTS = (4, 2)
+PARTS = (4, 1)
 ORDER = (2, 1, 3, 0)
 
 FAR_FIRST = [(j, i) for j in (2, 1, 3, 0) for i in (2, 1, 3, 0) if i + j > 0]
@@ -466,8 +466,8 @@
     forward(0)
     first_product(1, 1)
     sent(0, 2, 3)
-    send_rows(1, 0, 1, 0, KW // 2)
-    send_rows(1, 1, 3, 0, KW // 2)
+    send_rows(1, 0, 1)
+    send_rows(1, 1, 3)
     rep_copies = rep_third(rep_copies)
     product(1, 1)
     product(1, 3)
@@ -479,8 +479,6 @@
     sent(0, 4, 5)
     reduce_rows(0)
     grad_gain = send_norm(0, current, gain)
-    send_rows(1, 0, 1, 1, KW // 2)
-    send_rows(1, 1, 3, 1, KW // 2)
     send_rows(1, 2, 1)
     send_rows(1, 3, 3)
     forward(1)

time: 111 us -> 110 us (level)
  the two profiles are of different devices: /device:TPU:72 before, /device:TPU:1 now
where the time goes in v7:
time: 110 us; the launch traced here: 108 us
  Pallas kernels  104 us (95%)
  local copies, waits for them, and re-layouts  3.07 us (3%)
    pallas_call x1, Pallas kernels, window(): pl.pallas_call(kernel, out_shape=(jax.ShapeDtypeStruct((ROWS, KW), f32),...  104 us
    unnamed x2, local copies, waits for them, and re-layouts  3.07 us

profile of v7, /device:TPU:1, one launch (start us, length us, event | category | flops | bytes accessed | tf_op | source)
XLA Modules:
  0.0 107.9 jit_solution(5620530671121803011)
XLA Ops:
  0.6 104.2 %inner_window.1 = (f32[256,512]{1,0:T(8,128)}, f32[1,256]{1,0:T(1,128)}) custom-call(bf16[2,128,4096]{2,1,0:T(8,128)(2,1)} %inputs.1, bf16[2,128,512]{2,1,0:T(8,128)(2,1)} %cotangent.1, f32[256,512]{1,0:T(8,128)} %bitcast.7, bf16[256,512]{1,0:T(8,128)(2,1)} %bitcast.8, bf16[256,512]{1,0:T(8,128)(2,1)} %bitcast.9, f32[256,512]{1,0:T(8,128)} %anchor_weight.1, ...), custom_call_target="tpu_custom_call" | custom-call | flops 2147483648 | bytes 8388608 | tf_op jit(solution)/shard_map/inner_window/pallas_call | solution.py:521
  104.9 1.9 %copy.16 = f32[1,256,512]{2,1,0:T(8,128)} copy(f32[1,256,512]{2,1,0:T(8,128)} %bitcast.6) | data formatting | bytes 1048576
  106.7 1.2 %copy.17 = f32[1,256]{1,0:T(1,128)} copy(f32[1,256]{1,0:T(1,128)} %get-tuple-element.9) | data formatting | bytes 2048
